TPU v7x, 512 devices: a whole 4x4x16 slice. The times are simulated.
512 devices in a mesh: rep: 32 (over z, x_lo), gz: 16 (over x_hi, y, core).
Axes of the slice: x: 4 (x_hi: 2, x_lo: 2; x = x_hi * 2 + x_lo), y: 4, z: 16, core: 2. Of those that a mesh axis runs over, the one named last changes fastest.
Arguments:
- lattice_field: float32 [192, 64, 4096], P('rep', 'gz'), may hold values from -4 to 4
- langevin_noise: float32 [2, 192, 64, 4096], P(None, 'rep', 'gz'), may hold values from -5 to 5
- masses: float32 [64, 4096], P('gz'), may hold values from -2 to 2
- counts: int32 [192], replicated, may hold values from 0 to 49, as said below
- dest_slots: int32 [192], replicated, may hold values from 0 to 191, each once
- mode_bins: int32 [64, 64, 33], P('gz'), may hold values from 0 to 15, as said below
Outputs:
- resampled: float32 [192, 64, 4096], P('rep', 'gz')
- propagator: float32 [192, 16], P('rep')
Inputs may be any that keep to these rules, and one draw needn't show every extreme that they name: The counts sum to 192; in each aligned block of 6 replicas (those of one index of rep) at most 3 counts are nonzero, and exactly 3 in some block. `dest_slots`: A permutation of the 192 slots. `mode_bins`: the bin depends only on n_y^2 + n_z^2 + kx^2 with n = min(k, 64 - k), and never falls as that grows; every bin holds at least one mode.
All inputs are finite; a program needn't handle non-finite values.
Results may differ from a plain program's by a relative error of at most 0.00007.
Values sent between devices are 32-bit elements; how exact they have to be, the bound alone decides.
No kernel may reach another device: no remote copies, remote signals or barrier semaphores. Data moves between devices by JAX's collectives and lax.ppermute only.
A program may use at most 64 MiB of HBM per device.

v0:
```python
import jax
import jax.numpy as jnp
from jax import lax
from jax.sharding import PartitionSpec as P

L = 64
SWEEPS = 2
NBINS = 16
step_size = 0.1
quartic = 0.5


def with_halo(block, sides, width):
    for axis, dim in sides:
        count = lax.axis_size(axis)
        forward = [(i, i + 1) for i in range(count - 1)]
        forward.append((count - 1, 0))
        backward = [(target, source) for source, target in forward]
        low = lax.ppermute(
            lax.slice_in_dim(block, block.shape[dim] - width, None, axis=dim), axis, forward
        )
        high = lax.ppermute(lax.slice_in_dim(block, 0, width, axis=dim), axis, backward)
        block = jnp.concatenate([low, block, high], axis=dim)
    return block


def in_plane(center):
    grid = center.reshape(center.shape[0], center.shape[1], L, L)
    across = jnp.roll(grid, 1, axis=3) + jnp.roll(grid, -1, axis=3)
    return jnp.roll(center, L, axis=2) + jnp.roll(center, -L, axis=2) + across.reshape(center.shape)


def update(center, below, above, site_masses, noise_now):
    beside = below + above + in_plane(center)
    drift = 6.0 * center - beside + site_masses[None] * center + quartic * center * center * center
    return center - step_size * drift + jnp.sqrt(2.0 * step_size) * noise_now


def angle_tables(rows, columns):
    product = jnp.arange(rows)[:, None] * jnp.arange(columns)[None, :] % L
    theta = 2.0 * jnp.pi / L * product.astype(jnp.float32)
    return (jnp.cos(theta), jnp.sin(theta))


def make_weights(mode_bins):
    half = L // 2 + 1
    ordered = jnp.transpose(mode_bins, (1, 0, 2))
    wave_x = jnp.arange(half)
    weight_x = jnp.where((wave_x == 0) | (wave_x == L // 2), 1.0, 2.0).astype(jnp.float32)
    onehot = (ordered[..., None] == jnp.arange(NBINS)[None, None, None, :]).astype(jnp.float32)
    return (onehot * weight_x[None, None, :, None]).reshape(-1, NBINS)


def transform(slabs, weights):
    half = L // 2 + 1
    exact = lax.Precision.HIGHEST
    cos_half, sin_half = angle_tables(L, half)
    cos_full, sin_full = angle_tables(L, L)
    along_x = jnp.concatenate([cos_half, -sin_half], axis=1)
    count, depth = (slabs.shape[0], slabs.shape[1])
    grid = slabs.reshape(count, depth, L, L)
    first = jnp.einsum("nzyx,xk->nzyk", grid, along_x, precision=exact)
    real_x, imag_x = (first[..., :half], first[..., half:])
    real_y = jnp.einsum("qy,nzyk->nzqk", cos_full, real_x, precision=exact) + jnp.einsum(
        "qy,nzyk->nzqk", sin_full, imag_x, precision=exact
    )
    imag_y = jnp.einsum("qy,nzyk->nzqk", cos_full, imag_x, precision=exact) - jnp.einsum(
        "qy,nzyk->nzqk", sin_full, real_x, precision=exact
    )
    merged = jnp.concatenate([real_y, imag_y], axis=3).reshape(count, depth, L * 2 * half)
    block = lax.all_to_all(merged, "gz", split_axis=2, concat_axis=1, tiled=True)
    items = block.shape[0]
    pencil = block.reshape(items, L, -1, 2 * half)
    real_p = pencil[..., :half]
    imag_p = pencil[..., half:]
    real_z = jnp.einsum("pz,mzqk->mpqk", cos_full, real_p, precision=exact) + jnp.einsum(
        "pz,mzqk->mpqk", sin_full, imag_p, precision=exact
    )
    imag_z = jnp.einsum("pz,mzqk->mpqk", cos_full, imag_p, precision=exact) - jnp.einsum(
        "pz,mzqk->mpqk", sin_full, real_p, precision=exact
    )
    power = real_z * real_z + imag_z * imag_z
    binned = jnp.dot(power.reshape(items, -1), weights, precision=exact)
    binned_total, weight_total = lax.psum((binned, jnp.sum(weights, axis=0)), "gz")
    return binned_total / (float(L**3) * weight_total)


def local(lattice_field, langevin_noise, masses, counts, dest_slots, mode_bins):
    local_count = lattice_field.shape[0]
    weights = make_weights(mode_bins)
    swept = lattice_field
    for turn in range(SWEEPS):
        padded = with_halo(swept, (("gz", 1),), 1)
        swept = update(padded[:, 1:-1], padded[:, :-2], padded[:, 2:], masses, langevin_noise[turn])
    base = lax.axis_index("rep") * local_count
    ends = jnp.cumsum(counts)
    position = jnp.argsort(dest_slots)
    mine_position = lax.dynamic_slice_in_dim(position, base, local_count)
    mine_source = jnp.sum((ends[None, :] <= mine_position[:, None]).astype(jnp.int32), axis=1)
    empty = jnp.zeros_like(swept)
    piece = lax.all_gather(swept, "rep", axis=0, tiled=True)
    found = (mine_source >= 0) & (mine_source < piece.shape[0])
    chosen = jnp.take(piece, jnp.clip(mine_source, 0, piece.shape[0] - 1), axis=0)
    resampled = jnp.where(found[:, None, None], chosen, empty)
    propagator = transform(resampled, weights)
    return (resampled, propagator)


def solution(mesh):
    in_specs = (
        P("rep", "gz", None),
        P(None, "rep", "gz", None),
        P("gz", None),
        P(),
        P(),
        P("gz", None, None),
    )
    out_specs = (P("rep", "gz", None), P("rep", None))
    return jax.shard_map(local, mesh=mesh, in_specs=in_specs, out_specs=out_specs, check_vma=False)
```

profile of v0, /device:TPU:38, one launch (start us, length us, event | category | flops | bytes accessed | tf_op | source)
XLA Modules:
  0.0 452.3 jit_solution(2166895266252879648)
XLA Ops:
  7.2 1.3 fusion.124
  8.5 1.9 collective-permute-start
  10.4 7.3 %collective-permute-start.1 = (f32[6,1,4096]{2,1,0:T(1,128)S(1)}, f32[6,1,4096]{2,1,0:T(1,128)S(1)}, u32[]{:S(2)}, u32[]{:S(2)}) collective-permute-start(f32[6,1,4096]{2,1,0:T(1,128)S(1)} %get-tuple-element.27), channel_id=1, source_target_pairs={{1,0},{2,1},{3,2},{4,3},{5,4},{6,5},{7,6},{8,7},{9,8},{10,9},{11,1... | collective-permute-start | bytes 294920 | tf_op jit(solution)/shard_map/ppermute | solution.py:22
  17.7 1.4 reshape.93
  19.1 0.3 fusion.117
  19.4 0.3 fusion.118
  19.7 0.7 copy-done
  20.4 0.3 fusion.122
  20.7 0.7 fusion.123
  21.3 0.5 maximum_add_fusion
  21.8 0.3 add.129
  22.2 0.6 copy-done.4
  22.8 0.1 copy-done.1
  23.0 1.8 fusion.23
  24.7 0.4 reshape.94
  25.1 0.3 fusion.116
  25.4 0.3 fusion.115
  25.7 0.3 fusion.119
  26.0 0.8 fusion.121
  26.9 0.1 fusion.120
  26.9 1.9 collective-permute-start.2
  28.8 7.4 %collective-permute-start.3 = (f32[6,1,4096]{2,1,0:T(1,128)}, f32[6,1,4096]{2,1,0:T(1,128)S(1)}, u32[]{:S(2)}, u32[]{:S(2)}) collective-permute-start(f32[6,1,4096]{2,1,0:T(1,128)} %get-tuple-element.21), channel_id=1, source_target_pairs={{1,0},{2,1},{3,2},{4,3},{5,4},{6,5},{7,6},{8,7},{9,8},{10,9},{11,1... | collective-permute-start | bytes 294920 | tf_op jit(solution)/shard_map/ppermute | solution.py:22
  36.3 0.5 maximum_add_fusion.1
  36.8 0.3 add.138
  37.1 1.5 collective-permute-done.3
  38.6 1.6 fusion.27
  40.2 0.1 copy.56
  40.4 0.3 reduce-window.9
  40.9 0.2 mul.221
  41.1 0.2 eq.57
  41.3 3.2 sort.17
  44.6 0.1 slice_reduce_fusion
  44.8 0.2 convert_reduce_fusion
  45.0 0.1 sine_negate_fusion
  45.1 0.2 select_reduce_fusion
  45.3 281.6 %all-gather.2.cloned.1.call-done = f32[192,4,4096]{2,1,0:T(4,128)} async-done(((f32[6,4,4096]{2,1,0:T(4,128)}), f32[192,4,4096]{2,1,0:T(4,128)}) %all-gather.2.cloned.1.call-update) | async-done | bytes 12582928 | tf_op jit(solution)/shard_map/all_gather | solution.py:101
  326.9 5.4 %gather_fusion = f32[6,4,4096]{2,1,0:T(4,128)S(1)} fusion(f32[192,4,4096]{2,1,0:T(4,128)} %all-gather.2.cloned.1.call-done, s32[1024]{0:T(1024)S(1)} %pad_clamp_fusion), kind=kCustom, calls=%fused_computation | custom fusion | bytes 786456 | tf_op jit(solution)/shard_map/jit(_take)/gather | solution.py:103
  332.3 0.4 gather.7
  332.7 0.8 fusion.7
  333.5 1.4 fusion.14
  335.0 1.6 fusion.10
  336.6 1.6 fusion.5
  338.2 1.4 fusion.4
  339.6 0.1 pad_maximum_fusion
  339.7 9.3 %copy.65 = f32[6,4,64,66]{0,1,3,2:T(4,128)} copy(f32[6,4,64,66]{2,3,1,0:T(8,128)S(1)} %pad_maximum_fusion) | data formatting | bytes 811008 | tf_op jit(solution)/shard_map/reshape | solution.py:70
  349.0 12.4 %reshape.110 = f32[16,1,6336]{2,1,0:T(1,128)} reshape(f32[4224,4,6]{2,1,0:T(4,128)} %bitcast.64) | data formatting | bytes 811008
  361.4 7.3 %all-to-all-start = ((f32[16,1,6336]{2,1,0:T(1,128)}), f32[16,1,6336]{2,1,0:T(1,128)S(1)}, u32[]{:S(2)}, u32[]{:S(2)}) async-start(f32[16,1,6336]{2,1,0:T(1,128)} %reshape.110), calls=%async_computation | async-start | bytes 819200 | tf_op jit(solution)/shard_map/all_to_all | solution.py:71
  368.7 0.9 select_select_fusion
  369.6 7.4 %all-to-all-done = f32[16,1,6336]{2,1,0:T(1,128)S(1)} async-done(((f32[16,1,6336]{2,1,0:T(1,128)}), f32[16,1,6336]{2,1,0:T(1,128)S(1)}, u32[]{:S(2)}, u32[]{:S(2)}) %all-to-all-start) | async-done | bytes 405536 | tf_op jit(solution)/shard_map/all_to_all | solution.py:71
  376.9 0.5 broadcast.218
  377.5 1.6 reduce.2
  379.1 15.2 %reshape.111 = f32[4224,4,6]{2,1,0:T(4,128)} reshape(f32[16,6336]{1,0:T(8,128)S(1)} %reduce.2) | data formatting | bytes 811008
  394.3 7.6 %copy.51 = f32[6,4,16,264]{3,1,2,0:T(4,128)S(1)} copy(f32[6,4,16,264]{0,1,3,2:T(4,128)} %bitcast.65) | data formatting | bytes 811008 | tf_op jit(solution)/shard_map/all_to_all | solution.py:71
  401.9 0.6 reshape.96
  402.5 0.5 fusion.114
  402.9 0.3 copy.67
  403.3 0.7 fusion.56
  404.0 0.3 copy.68
  404.3 0.7 fusion.54
  405.0 0.7 fusion.3
  405.7 0.7 fusion.2
  406.4 1.6 convolution_bitcast_fusion
  407.9 36.9 %all-reduce.1 = (f32[6,16]{1,0:T(8,128)S(1)}, f32[16]{0:T(128)S(1)}) all-reduce(f32[6,16]{1,0:T(8,128)S(1)} %convolution_bitcast_fusion, f32[16]{0:T(128)S(1)} %select_reduce_fusion), channel_id=1, replica_groups=mesh['rep'=32,'gz'=16] {'gz'}, use_global_device_ids=true, to_apply=%region_4.5 | all-reduce | flops 112 | bytes 896 | tf_op jit(solution)/shard_map/psum | solution.py:84
  444.9 0.6 broadcast_divide_fusion
  (31 shorter events, 0.5 us)
Async XLA Ops:
  7.2 319.8 %all-gather.2.cloned.1.call-start = ((), (), s32[]{:S(2)}) async-start(), calls=%async_computation.1 | async-start | bytes 12976128 | tf_op jit(solution)/shard_map/all_gather | solution.py:101
  8.5 13.6 %collective-permute-start = (f32[6,1,4096]{2,1,0:T(1,128)S(1)}, f32[6,1,4096]{2,1,0:T(1,128)S(1)}, u32[]{:S(2)}, u32[]{:S(2)}) collective-permute-start(f32[6,1,4096]{2,1,0:T(1,128)S(1)} %get-tuple-element.26), channel_id=1, source_target_pairs={{0,1},{1,2},{2,3},{3,4},{4,5},{5,6},{6,7},{7,8},{8,9},{9,10},{10,1... | collective-permute-start | bytes 294920 | tf_op jit(solution)/shard_map/ppermute | solution.py:19
  10.4 11.7 %collective-permute-start.1 = (f32[6,1,4096]{2,1,0:T(1,128)S(1)}, f32[6,1,4096]{2,1,0:T(1,128)S(1)}, u32[]{:S(2)}, u32[]{:S(2)}) collective-permute-start(f32[6,1,4096]{2,1,0:T(1,128)S(1)} %get-tuple-element.27), channel_id=1, source_target_pairs={{1,0},{2,1},{3,2},{4,3},{5,4},{6,5},{7,6},{8,7},{9,8},{10,9},{11,1... | collective-permute-start | bytes 294920 | tf_op jit(solution)/shard_map/ppermute | solution.py:22
  19.4 1.0 copy-start
  21.8 1.1 copy-start.1
  22.2 0.6 copy-start.4
  22.2 0.7 copy-start.5
  26.9 10.2 %collective-permute-start.2 = (f32[6,1,4096]{2,1,0:T(1,128)}, f32[6,1,4096]{2,1,0:T(1,128)S(1)}, u32[]{:S(2)}, u32[]{:S(2)}) collective-permute-start(f32[6,1,4096]{2,1,0:T(1,128)} %get-tuple-element.20), channel_id=1, source_target_pairs={{0,1},{1,2},{2,3},{3,4},{4,5},{5,6},{6,7},{7,8},{8,9},{9,10},{10,1... | collective-permute-start | bytes 294920 | tf_op jit(solution)/shard_map/ppermute | solution.py:19
  28.8 9.8 %collective-permute-start.3 = (f32[6,1,4096]{2,1,0:T(1,128)}, f32[6,1,4096]{2,1,0:T(1,128)S(1)}, u32[]{:S(2)}, u32[]{:S(2)}) collective-permute-start(f32[6,1,4096]{2,1,0:T(1,128)} %get-tuple-element.21), channel_id=1, source_target_pairs={{1,0},{2,1},{3,2},{4,3},{5,4},{6,5},{7,6},{8,7},{9,8},{10,9},{11,1... | collective-permute-start | bytes 294920 | tf_op jit(solution)/shard_map/ppermute | solution.py:22
  36.8 1.9 copy-start.3
  38.6 1.6 copy-start.2
  38.6 1.8 copy-start.6
  40.2 1.1 copy-start.7
  361.4 15.5 %all-to-all-start = ((f32[16,1,6336]{2,1,0:T(1,128)}), f32[16,1,6336]{2,1,0:T(1,128)S(1)}, u32[]{:S(2)}, u32[]{:S(2)}) async-start(f32[16,1,6336]{2,1,0:T(1,128)} %reshape.110), calls=%async_computation | async-start | bytes 819200 | tf_op jit(solution)/shard_map/all_to_all | solution.py:71
Sparse Core Ops, SparseCore 0:
  40.3 286.5 all-gather.1
where the time goes:
time: 453 us; the launch traced here: 452 us
  waiting for transfers between devices  290 us (64%)
  local copies, waits for them, and re-layouts  61.9 us (14%)
  blocking collectives  36.9 us (8%)
  starting transfers between devices  25.8 us (6%)
  between operations  14.4 us (3%)
  other arithmetic  11.6 us (3%)
  matrix products  11.2 us (2%)
    all_gather x1, waiting for transfers between devices, local(): piece = lax.all_gather(swept, 'rep', axis=0, tiled=True)  282 us
    psum x1, blocking collectives, transform(): lax.psum((binned, jnp.sum(weights, axis=0)), 'gz')  36.9 us
    unnamed x20, local copies, waits for them, and re-layouts  29.8 us
    ppermute x2, starting transfers between devices, with_halo(): lax.ppermute(lax.slice_in_dim(block, 0, width, axis=dim), axis, backward)  14.7 us
    reshape x1, local copies, waits for them, and re-layouts, transform(): jnp.concatenate([real_y, imag_y], axis=3)  9.27 us
  transfers between devices with their start and end apart: 6, of which 3 were waited for; matrix products, arithmetic and copies ran while one was open for 2% of the time, Pallas kernels for 0%

commit v1 on v0

--- a/solution.py
+++ b/solution.py
@@ -98,7 +98,8 @@
     mine_position = lax.dynamic_slice_in_dim(position, base, local_count)
     mine_source = jnp.sum((ends[None, :] <= mine_position[:, None]).astype(jnp.int32), axis=1)
     empty = jnp.zeros_like(swept)
-    piece = lax.all_gather(swept, "rep", axis=0, tiled=True)
+    sent = jnp.stack([swept] * lax.axis_size("rep"))
+    piece = jnp.concatenate(lax.all_to_all(sent, "rep", 0, 0), axis=0)
     found = (mine_source >= 0) & (mine_source < piece.shape[0])
     chosen = jnp.take(piece, jnp.clip(mine_source, 0, piece.shape[0] - 1), axis=0)
     resampled = jnp.where(found[:, None, None], chosen, empty)

time: 453 us -> 722 us (1.59)
  the two profiles are of different devices: /device:TPU:38 before, /device:TPU:6 now
where the time goes in v1:
time: 722 us; the launch traced here: 721 us
  waiting for transfers between devices  546 us (76%)
  local copies, waits for them, and re-layouts  69.3 us (10%)
  starting transfers between devices  45 us (6%)
  blocking collectives  36.9 us (5%)
  matrix products  11.2 us (2%)
  other arithmetic  10.9 us (2%)
    all_to_all x1, waiting for transfers between devices, local(): piece = jnp.concatenate(lax.all_to_all(sent, 'rep', 0, 0), axis=0)  538 us
    psum x1, blocking collectives, transform(): lax.psum((binned, jnp.sum(weights, axis=0)), 'gz')  36.9 us
    unnamed x20, local copies, waits for them, and re-layouts  29.8 us
    all_to_all x1, starting transfers between devices, local(): piece = jnp.concatenate(lax.all_to_all(sent, 'rep', 0, 0), axis=0)  16.9 us
    ppermute x2, starting transfers between devices, with_halo(): lax.ppermute(lax.slice_in_dim(block, 0, width, axis=dim), axis, backward)  14.5 us
  transfers between devices with their start and end apart: 6, of which 3 were waited for; matrix products, arithmetic and copies ran while one was open for 1% of the time, Pallas kernels for 0%

profile of v1, /device:TPU:6, one launch (start us, length us, event | category | flops | bytes accessed | tf_op | source)
XLA Modules:
  0.0 720.7 jit_solution(12837699114552143509)
XLA Ops:
  0.6 1.3 fusion.124
  1.9 1.9 collective-permute-start
  3.9 7.3 %collective-permute-start.1 = (f32[6,1,4096]{2,1,0:T(1,128)S(1)}, f32[6,1,4096]{2,1,0:T(1,128)S(1)}, u32[]{:S(2)}, u32[]{:S(2)}) collective-permute-start(f32[6,1,4096]{2,1,0:T(1,128)S(1)} %get-tuple-element.27), channel_id=1, source_target_pairs={{1,0},{2,1},{3,2},{4,3},{5,4},{6,5},{7,6},{8,7},{9,8},{10,9},{11,1... | collective-permute-start | bytes 294920 | tf_op jit(solution)/shard_map/ppermute | solution.py:22
  11.1 1.4 reshape.98
  12.5 0.3 fusion.117
  12.8 0.3 fusion.118
  13.1 0.7 copy-done
  13.8 0.3 fusion.122
  14.1 0.7 fusion.123
  14.8 0.5 maximum_add_fusion
  15.3 0.3 add.129
  15.6 0.6 copy-done.4
  16.3 0.1 copy-done.1
  16.4 1.8 fusion.23
  18.1 0.4 reshape.99
  18.6 0.3 fusion.116
  18.9 0.3 fusion.115
  19.1 0.3 fusion.119
  19.4 0.8 fusion.121
  20.3 1.9 collective-permute-start.2
  22.2 7.3 %collective-permute-start.3 = (f32[6,1,4096]{2,1,0:T(1,128)S(1)}, f32[6,1,4096]{2,1,0:T(1,128)S(1)}, u32[]{:S(2)}, u32[]{:S(2)}) collective-permute-start(f32[6,1,4096]{2,1,0:T(1,128)S(1)} %get-tuple-element.21), channel_id=1, source_target_pairs={{1,0},{2,1},{3,2},{4,3},{5,4},{6,5},{7,6},{8,7},{9,8},{10,9},{11,1... | collective-permute-start | bytes 294920 | tf_op jit(solution)/shard_map/ppermute | solution.py:22
  29.5 0.5 maximum_add_fusion.1
  30.0 0.3 add.138
  30.3 1.4 collective-permute-done.3
  31.7 0.8 fusion.27
  32.5 7.6 %stack.2 = f32[32,6,4,4096]{3,2,1,0:T(4,128)} broadcast(f32[6,4,4096]{2,1,0:T(4,128)S(1)} %fusion.27), dimensions={1,2,3} | broadcast | bytes 12976128 | tf_op jit(solution)/shard_map/stack | solution.py:101
  40.1 16.9 %all-to-all-start = ((f32[32,6,4,4096]{3,2,1,0:T(4,128)}), f32[32,6,4,4096]{3,2,1,0:T(4,128)}, u32[]{:S(2)}, u32[]{:S(2)}) async-start(f32[32,6,4,4096]{3,2,1,0:T(4,128)} %stack.2), calls=%async_computation | async-start | bytes 25165824 | tf_op jit(solution)/shard_map/all_to_all | solution.py:102
  57.1 0.1 copy.56
  57.2 0.3 reduce-window.9
  57.7 0.2 mul.221
  57.9 0.2 eq.57
  58.2 3.2 sort.17
  61.4 0.1 slice_reduce_fusion
  61.6 0.2 convert_reduce_fusion
  61.8 0.1 sine_negate_fusion
  61.9 0.2 select_reduce_fusion
  62.2 537.6 %all-to-all-done = f32[32,6,4,4096]{3,2,1,0:T(4,128)} async-done(((f32[32,6,4,4096]{3,2,1,0:T(4,128)}), f32[32,6,4,4096]{3,2,1,0:T(4,128)}, u32[]{:S(2)}, u32[]{:S(2)}) %all-to-all-start) | async-done | bytes 12582944 | tf_op jit(solution)/shard_map/all_to_all | solution.py:102
  599.8 5.4 gather_fusion
  605.2 0.4 gather.7
  605.6 0.8 fusion.7
  606.4 1.4 fusion.14
  607.8 1.6 fusion.10
  609.5 1.6 fusion.5
  611.1 1.4 fusion.4
  612.6 9.1 %copy.65 = f32[6,4,64,66]{0,1,3,2:T(4,128)} copy(f32[6,4,64,66]{2,3,1,0:T(8,128)S(1)} %pad_maximum_fusion) | data formatting | bytes 811008 | tf_op jit(solution)/shard_map/reshape | solution.py:70
  621.8 12.4 %reshape.116 = f32[16,1,6336]{2,1,0:T(1,128)} reshape(f32[4224,4,6]{2,1,0:T(4,128)} %bitcast.65) | data formatting | bytes 811008
  634.2 9.7 %all-to-all-start.1 = ((f32[16,1,6336]{2,1,0:T(1,128)}), f32[16,1,6336]{2,1,0:T(1,128)S(1)}, u32[]{:S(2)}, u32[]{:S(2)}) async-start(f32[16,1,6336]{2,1,0:T(1,128)} %reshape.116), calls=%async_computation.1 | async-start | bytes 819200 | tf_op jit(solution)/shard_map/all_to_all | solution.py:71
  643.9 0.9 select_select_fusion
  644.8 7.4 %all-to-all-done.1 = f32[16,1,6336]{2,1,0:T(1,128)S(1)} async-done(((f32[16,1,6336]{2,1,0:T(1,128)}), f32[16,1,6336]{2,1,0:T(1,128)S(1)}, u32[]{:S(2)}, u32[]{:S(2)}) %all-to-all-start.1) | async-done | bytes 405536 | tf_op jit(solution)/shard_map/all_to_all | solution.py:71
  652.2 0.5 broadcast.220
  652.7 1.6 reduce.2
  654.3 15.2 %reshape.117 = f32[4224,4,6]{2,1,0:T(4,128)} reshape(f32[16,6336]{1,0:T(8,128)S(1)} %reduce.2) | data formatting | bytes 811008
  669.5 7.6 %copy.51 = f32[6,4,16,264]{3,1,2,0:T(4,128)S(1)} copy(f32[6,4,16,264]{0,1,3,2:T(4,128)} %bitcast.66) | data formatting | bytes 811008 | tf_op jit(solution)/shard_map/all_to_all | solution.py:71
  677.1 0.6 reshape.102
  677.7 0.5 fusion.114
  678.2 0.3 copy.67
  678.5 0.7 fusion.56
  679.2 0.3 copy.68
  679.5 0.7 fusion.54
  680.2 0.7 fusion.3
  680.9 0.7 fusion.2
  681.6 1.6 convolution_bitcast_fusion
  683.2 36.9 %all-reduce.1 = (f32[6,16]{1,0:T(8,128)S(1)}, f32[16]{0:T(128)S(1)}) all-reduce(f32[6,16]{1,0:T(8,128)S(1)} %convolution_bitcast_fusion, f32[16]{0:T(128)S(1)} %select_reduce_fusion), channel_id=1, replica_groups=mesh['rep'=32,'gz'=16] {'gz'}, use_global_device_ids=true, to_apply=%region_4.5 | all-reduce | flops 112 | bytes 896 | tf_op jit(solution)/shard_map/psum | solution.py:84
  720.1 0.6 broadcast_divide_fusion
  (31 shorter events, 0.6 us)
Async XLA Ops:
  1.9 13.6 %collective-permute-start = (f32[6,1,4096]{2,1,0:T(1,128)S(1)}, f32[6,1,4096]{2,1,0:T(1,128)S(1)}, u32[]{:S(2)}, u32[]{:S(2)}) collective-permute-start(f32[6,1,4096]{2,1,0:T(1,128)S(1)} %get-tuple-element.26), channel_id=1, source_target_pairs={{0,1},{1,2},{2,3},{3,4},{4,5},{5,6},{6,7},{7,8},{8,9},{9,10},{10,1... | collective-permute-start | bytes 294920 | tf_op jit(solution)/shard_map/ppermute | solution.py:19
  3.9 11.7 %collective-permute-start.1 = (f32[6,1,4096]{2,1,0:T(1,128)S(1)}, f32[6,1,4096]{2,1,0:T(1,128)S(1)}, u32[]{:S(2)}, u32[]{:S(2)}) collective-permute-start(f32[6,1,4096]{2,1,0:T(1,128)S(1)} %get-tuple-element.27), channel_id=1, source_target_pairs={{1,0},{2,1},{3,2},{4,3},{5,4},{6,5},{7,6},{8,7},{9,8},{10,9},{11,1... | collective-permute-start | bytes 294920 | tf_op jit(solution)/shard_map/ppermute | solution.py:22
  12.8 1.0 copy-start
  15.2 1.1 copy-start.1
  15.6 0.6 copy-start.4
  15.6 0.7 copy-start.5
  20.3 10.0 %collective-permute-start.2 = (f32[6,1,4096]{2,1,0:T(1,128)}, f32[6,1,4096]{2,1,0:T(1,128)S(1)}, u32[]{:S(2)}, u32[]{:S(2)}) collective-permute-start(f32[6,1,4096]{2,1,0:T(1,128)} %get-tuple-element.20), channel_id=1, source_target_pairs={{0,1},{1,2},{2,3},{3,4},{4,5},{5,6},{6,7},{7,8},{8,9},{9,10},{10,1... | collective-permute-start | bytes 294920 | tf_op jit(solution)/shard_map/ppermute | solution.py:19
  22.2 9.5 %collective-permute-start.3 = (f32[6,1,4096]{2,1,0:T(1,128)S(1)}, f32[6,1,4096]{2,1,0:T(1,128)S(1)}, u32[]{:S(2)}, u32[]{:S(2)}) collective-permute-start(f32[6,1,4096]{2,1,0:T(1,128)S(1)} %get-tuple-element.21), channel_id=1, source_target_pairs={{1,0},{2,1},{3,2},{4,3},{5,4},{6,5},{7,6},{8,7},{9,8},{10,9},{11,1... | collective-permute-start | bytes 294920 | tf_op jit(solution)/shard_map/ppermute | solution.py:22
  30.0 1.7 copy-start.3
  40.1 16.9 %copy-start.2 = (s32[4,64,33]{1,0,2:T(4,128)S(1)}, s32[4,64,33]{1,0,2:T(4,128)}, u32[]{:S(2)}) copy-start(s32[4,64,33]{1,0,2:T(4,128)} %param.11) | copy-start | bytes 101380
  40.1 17.1 %copy-start.6 = (s32[192]{0:T(256)S(1)}, s32[192]{0:T(256)}, u32[]{:S(2)}) copy-start(s32[192]{0:T(256)} %param.9) | copy-start | bytes 2308
  40.1 18.0 %copy-start.7 = (s32[192]{0:T(256)S(1)}, s32[192]{0:T(256)}, u32[]{:S(2)}) copy-start(s32[192]{0:T(256)} %param.10) | copy-start | bytes 2308
  40.1 559.7 %all-to-all-start = ((f32[32,6,4,4096]{3,2,1,0:T(4,128)}), f32[32,6,4,4096]{3,2,1,0:T(4,128)}, u32[]{:S(2)}, u32[]{:S(2)}) async-start(f32[32,6,4,4096]{3,2,1,0:T(4,128)} %stack.2), calls=%async_computation | async-start | bytes 25165824 | tf_op jit(solution)/shard_map/all_to_all | solution.py:102
  634.2 18.0 %all-to-all-start.1 = ((f32[16,1,6336]{2,1,0:T(1,128)}), f32[16,1,6336]{2,1,0:T(1,128)S(1)}, u32[]{:S(2)}, u32[]{:S(2)}) async-start(f32[16,1,6336]{2,1,0:T(1,128)} %reshape.116), calls=%async_computation.1 | async-start | bytes 819200 | tf_op jit(solution)/shard_map/all_to_all | solution.py:71
